TPU v7x, 256 devices: a whole 4x4x8 slice. The times are simulated.
256 devices in a mesh: dp: 32 (over x, y, core), seq: 8 (over z).
Axes of the slice: x: 4, y: 4, z: 8, core: 2. Of those that a mesh axis runs over, the one named last changes fastest.
Arguments:
- latents: bfloat16 [224, 8, 64, 1152], P('dp', 'seq'), may hold values from -7 to 7
- w_spatial_qkv: bfloat16 [1152, 1728], replicated, may hold values from -1 to 1
- w_spatial_out: bfloat16 [576, 1152], replicated, may hold values from -0.25 to 0.25
- w_temporal_qkv: bfloat16 [1152, 1728], replicated, may hold values from -1 to 1
- w_temporal_out: bfloat16 [576, 1152], replicated, may hold values from -0.25 to 0.25
- spatial_len: int32 [224], replicated, may hold values from 16 to 64, as said below
- frames_len: int32 [224], replicated, may hold values from 1 to 8
- target: int32 [224], replicated, may hold values from 0 to 223, as said below
Outputs:
- blended: bfloat16 [224, 8, 64, 1152], P('dp', 'seq')
Inputs may be any that keep to these rules, and one draw needn't show every extreme that they name: `spatial_len`: each clip's bucket holds 16, 32, 48 or 64 tokens. `target`: a permutation of the clip slots; clip slot c of group g goes to slot c of some group; the 7 clips of a group go to 7 different groups, so a group sends exactly one clip to each of 7 groups and receives 7 clips.
All inputs are finite; a program needn't handle non-finite values.
Results may differ from a plain program's by a relative error of at most 0.019.
Values may be sent and summed in bfloat16 or wider, within the bound.
No kernel may reach another device: no remote copies, remote signals or barrier semaphores. Data moves between devices by JAX's collectives and lax.ppermute only.
A program may use at most 128 MiB of HBM per device.

v0:
```python
import jax
import jax.numpy as jnp
from jax import lax
from jax.sharding import PartitionSpec as P

HEADS = 8
HD = 72
HW = 576


def layer_norm(values):
    wide = values.astype(jnp.float32)
    centre = wide - jnp.mean(wide, axis=-1, keepdims=True)
    spread = jnp.mean(centre * centre, axis=-1, keepdims=True)
    return (centre * lax.rsqrt(spread + 1e-06)).astype(jnp.bfloat16)


def attend(query, keys, values, scores_form, out_form, live):
    scores = jnp.einsum(scores_form, query, keys, preferred_element_type=jnp.float32) * HD ** (-0.5)
    scores = jnp.where(live, scores, -1e30)
    probs = jax.nn.softmax(scores, axis=-1).astype(jnp.bfloat16)
    return jnp.einsum(out_form, probs, values, preferred_element_type=jnp.float32).astype(
        jnp.bfloat16
    )


def routing(target, width):
    group = lax.axis_index("dp")
    groups = lax.axis_size("dp")
    capacity = (width + groups - 1) // groups
    table = target.reshape(groups, width) // width
    mine = lax.dynamic_slice_in_dim(table, group, 1, 0)[0]
    column = jnp.arange(width, dtype=jnp.int32)
    earlier = (mine[None, :] == mine[:, None]) & (column[None, :] < column[:, None])
    rank = jnp.sum(earlier.astype(jnp.int32), axis=1)
    row_id = mine * capacity + rank
    select = (jnp.arange(groups * capacity, dtype=jnp.int32)[:, None] == row_id[None, :]).astype(
        jnp.bfloat16
    )
    wanted = group * width + column
    every = jnp.arange(groups * width, dtype=jnp.int32)
    match = target[None, :] == wanted[:, None]
    source = jnp.sum(jnp.where(match, every[None, :], 0), axis=1)
    src_group = source // width
    src_slot = source % width
    rows = table[src_group]
    rank_in = jnp.sum(
        ((rows == group) & (column[None, :] < src_slot[:, None])).astype(jnp.int32), axis=1
    )
    pick = src_group * capacity + rank_in
    home = group * width + column
    return (select, pick, source, home)


def pack_out(select, blocks):
    return jnp.einsum("rc,cfsd->rfsd", select, blocks, preferred_element_type=jnp.float32).astype(
        jnp.bfloat16
    )


def spatial_part(clips, w_spatial_qkv, w_spatial_out, slen):
    count, frames, slots, width = clips.shape
    normed = layer_norm(clips).reshape(-1, width)
    qkv = jnp.dot(normed, w_spatial_qkv, preferred_element_type=jnp.float32).astype(jnp.bfloat16)
    qkv = qkv.reshape(count, frames, slots, 3, HEADS, HD)
    live = (jnp.arange(slots)[None, :] < slen[:, None])[:, None, None, None, :]
    attn = attend(
        qkv[:, :, :, 0],
        qkv[:, :, :, 1],
        qkv[:, :, :, 2],
        "cfshe,cfthe->cfhst",
        "cfhst,cfthe->cfshe",
        live,
    )
    mid = clips.reshape(-1, width).astype(jnp.float32) + jnp.dot(
        attn.reshape(-1, HW), w_spatial_out, preferred_element_type=jnp.float32
    )
    return mid.astype(jnp.bfloat16).reshape(count, frames, slots, width)


def temporal_part(mid, w_temporal_qkv, w_temporal_out, flen):
    count, frames, slots, width = mid.shape
    qkv = jnp.dot(
        layer_norm(mid).reshape(-1, width), w_temporal_qkv, preferred_element_type=jnp.float32
    ).astype(jnp.bfloat16)
    qkv = qkv.reshape(count, frames, slots, 3, HW)
    keys, values = (
        lax.all_gather(qkv[:, :, :, 1], "seq", axis=1, tiled=True),
        lax.all_gather(qkv[:, :, :, 2], "seq", axis=1, tiled=True),
    )
    total = keys.shape[1]
    query = qkv[:, :, :, 0].reshape(count, frames, slots, HEADS, HD)
    keys = keys.reshape(count, total, slots, HEADS, HD)
    values = values.reshape(count, total, slots, HEADS, HD)
    live = (jnp.arange(total)[None, :] < flen[:, None])[:, None, None, None, :]
    attn = attend(query, keys, values, "cfshe,cgshe->cshfg", "cshfg,cgshe->cfshe", live)
    block = mid.reshape(-1, width).astype(jnp.float32) + jnp.dot(
        attn.reshape(-1, HW), w_temporal_out, preferred_element_type=jnp.float32
    )
    return block.astype(jnp.bfloat16).reshape(count, frames, slots, width)


def per_device(
    latents,
    w_spatial_qkv,
    w_spatial_out,
    w_temporal_qkv,
    w_temporal_out,
    spatial_len,
    frames_len,
    target,
):
    width = latents.shape[0]
    select, pick, source, home = routing(target, width)
    arrived = lax.all_to_all(
        pack_out(select, latents), "dp", split_axis=0, concat_axis=0, tiled=True
    )
    clips = jnp.take(arrived, pick, axis=0)
    mid = spatial_part(clips, w_spatial_qkv, w_spatial_out, spatial_len[source])
    return temporal_part(mid, w_temporal_qkv, w_temporal_out, frames_len[source])


def solution(mesh):
    return jax.shard_map(
        per_device,
        mesh=mesh,
        in_specs=(P("dp", "seq", None, None), P(), P(), P(), P(), P(), P(), P()),
        out_specs=P("dp", "seq", None, None),
        check_vma=False,
    )
```

profile of v0, /device:TPU:1, one launch (start us, length us, event | category | flops | bytes accessed | tf_op | source)
XLA Modules:
  0.0 280.6 jit_solution(5448329915507551470)
XLA Ops:
  8.5 2.7 fusion.7
  11.2 3.8 %copy.38 = bf16[32,1,64,1152]{3,2,1,0:T(8,128)(2,1)} copy(bf16[32,1,64,1152]{3,0,2,1:T(8,128)(2,1)S(1)} %fusion.7) | data formatting | bytes 9437184 | tf_op jit(solution)/shard_map/convert_element_type | solution.py:56
  15.0 8.8 %all-to-all-start = ((bf16[32,1,64,1152]{3,2,1,0:T(8,128)(2,1)}), bf16[32,1,64,1152]{3,2,1,0:T(8,128)(2,1)}, u32[]{:S(2)}, u32[]{:S(2)}) async-start(bf16[32,1,64,1152]{3,2,1,0:T(8,128)(2,1)} %copy.38), calls=%async_computation | async-start | bytes 9437184 | tf_op jit(solution)/shard_map/all_to_all | solution.py:115
  25.8 56.4 %all-to-all-done = bf16[32,1,64,1152]{3,2,1,0:T(8,128)(2,1)} async-done(((bf16[32,1,64,1152]{3,2,1,0:T(8,128)(2,1)}), bf16[32,1,64,1152]{3,2,1,0:T(8,128)(2,1)}, u32[]{:S(2)}, u32[]{:S(2)}) %all-to-all-start) | async-done | bytes 4718624 | tf_op jit(solution)/shard_map/all_to_all | solution.py:115
  82.2 3.0 %gather_fusion.1 = bf16[7,64,1152]{2,1,0:T(8,128)(2,1)S(1)} fusion(bf16[32,64,1152]{2,1,0:T(8,128)(2,1)} %bitcast.8, s32[1024]{0:T(1024)S(1)} %pad_clamp_fusion.1), kind=kCustom, calls=%fused_computation.1 | custom fusion | bytes 2064412 | tf_op jit(solution)/shard_map/jit(_take)/gather | solution.py:118
  87.5 4.5 %convolution_convert_fusion.2 = bf16[448,1728]{1,0:T(8,128)(2,1)S(1)} fusion(bf16[1152,1728]{0,1:T(8,128)(2,1)} %param.9, bf16[448,1152]{1,0:T(8,128)(2,1)S(1)} %bitcast_select_fusion.1, f32[448]{0:T(512)S(1)} %rsqrt.20, f32[448]{0:T(512)S(1)} %div.67), kind=kOutput, calls=%fused_computation.19 | convolution fusion | flops 1786466304 | bytes 6565376 | tf_op jit(solution)/shard_map/dot_general | solution.py:64
  92.0 4.2 %reshape.334 = bf16[7,1,64,3,8,72]{5,4,3,2,0,1:T(8,128)(2,1)} reshape(bf16[448,1728]{1,0:T(8,128)(2,1)S(1)} %convolution_convert_fusion.2) | data formatting | bytes 3096576 | tf_op jit(solution)/shard_map/reshape | solution.py:65
  96.1 2.9 %fusion.57 = (bf16[7,1,64,1,8,72]{5,4,3,2,0,1:T(8,128)(2,1)S(1)}, bf16[7,1,64,1,8,72]{5,4,3,2,0,1:T(8,128)(2,1)S(1)}, bf16[7,1,64,1,8,72]{5,4,3,2,0,1:T(8,128)(2,1)}) fusion(bf16[7,1,64,3,8,72]{5,4,3,2,0,1:T(8,128)(2,1)} %reshape.334), kind=kLoop, calls=%fused_computation.110 | loop fusion | bytes 3096576 | tf_op jit(solution)/shard_map/slice | solution.py:70
  99.0 3.4 %fusion.59 = (f32[7,8,64]{2,1,0:T(8,128)S(1)}, f32[7,8,64,64]{2,3,1,0:T(8,128)}) fusion(pred[7,64]{1,0:T(8,128)(4,1)S(1)} %iota_compare_fusion.1, bf16[7,1,64,1,8,72]{5,4,3,2,0,1:T(8,128)(2,1)} %get-tuple-element.7, bf16[7,1,64,1,8,72]{5,4,3,2,0,1:T(8,128)(2,1)S(1)} %get-tuple-element.6), kind=kOutput, calls=%fused_computation.112 | convolution fusion | flops 33947712 | bytes 1964480 | tf_op jit(solution)/shard_map/sub | solution.py:21
  102.5 2.0 fusion.19
  106.6 2.3 convert_reduce_fusion
  109.9 2.4 convolution_convert_fusion.1
  112.3 2.5 reshape.339
  114.7 7.7 %fusion.58 = (bf16[7,1,64,1,576]{4,3,2,0,1:T(2,128)(2,1)S(1)}, bf16[7,1,64,1,576]{4,3,2,0,1:T(2,128)(2,1)S(1)}, bf16[7,64,576]{2,1,0:T(8,128)(2,1)S(1)}) fusion(bf16[7,1,64,3,576]{4,3,2,0,1:T(4,128)(2,1)} %reshape.339), kind=kLoop, calls=%fused_computation.111 | loop fusion | bytes 3096576 | tf_op jit(solution)/shard_map/slice | solution.py:89
  125.0 4.0 %reshape.391 = bf16[7,64,8,72,1]{3,4,2,1,0:T(2,128)(2,1)} reshape(bf16[7,64,576]{2,1,0:T(8,128)(2,1)S(1)} %get-tuple-element.10) | data formatting | bytes 1032192 | tf_op jit(solution)/shard_map/reshape.29
  129.1 55.8 %all-gather.7.cloned.1.call-done = bf16[7,8,64,1,576]{4,2,3,0,1:T(8,128)(2,1)} async-done(((bf16[7,1,64,1,576]{4,2,3,0,1:T(8,128)(2,1)}), bf16[7,8,64,1,576]{4,2,3,0,1:T(8,128)(2,1)}) %all-gather.7.cloned.1.call-update) | async-done | bytes 4128784 | tf_op jit(solution)/shard_map/all_gather | solution.py:88
  185.0 12.5 %reshape.392 = bf16[7,8,64,8,72]{4,3,2,0,1:T(8,128)(2,1)} reshape(bf16[7,8,64,1,576]{4,2,3,0,1:T(8,128)(2,1)} %all-gather.7.cloned.1.call-done) | data formatting | bytes 8257536 | tf_op jit(solution)/shard_map/reshape | solution.py:93
  197.5 10.2 %fusion.3 = f32[7,64,8,1,8]{4,3,2,1,0:T(1,128)} fusion(bf16[7,64,8,72,1]{3,4,2,1,0:T(2,128)(2,1)S(1)} %copy-done.4, bf16[7,8,64,8,72]{4,3,2,0,1:T(8,128)(2,1)} %reshape.392), kind=kOutput, calls=%fused_computation.7 | convolution fusion | flops 4128768 | bytes 4759552 | tf_op jit(solution)/shard_map/cfshe,cgshe->cshfg/dot_general | solution.py:19
  207.7 4.3 %copy.52 = f32[7,64,8,1,8]{1,4,2,0,3:T(8,128)S(1)} copy(f32[7,64,8,1,8]{4,3,2,1,0:T(1,128)} %fusion.3) | data formatting | bytes 229376 | tf_op jit(solution)/shard_map/cfshe,cgshe->cshfg/dot_general | solution.py:19
  213.9 30.0 %all-gather.5.cloned.1.call-done = bf16[7,8,64,1,576]{4,2,3,0,1:T(8,128)(2,1)} async-done(((bf16[7,1,64,1,576]{4,2,3,0,1:T(8,128)(2,1)}), bf16[7,8,64,1,576]{4,2,3,0,1:T(8,128)(2,1)}) %all-gather.5.cloned.1.call-update) | async-done | bytes 4128784 | tf_op jit(solution)/shard_map/all_gather | solution.py:89
  243.9 12.5 %reshape.389 = bf16[7,8,64,8,72]{4,3,2,0,1:T(8,128)(2,1)} reshape(bf16[7,8,64,1,576]{4,2,3,0,1:T(8,128)(2,1)} %all-gather.5.cloned.1.call-done) | data formatting | bytes 8257536 | tf_op jit(solution)/shard_map/reshape | solution.py:94
  256.4 10.7 %fusion.5 = f32[7,64,8,1,72]{4,3,2,1,0:T(1,128)} fusion(bf16[7,64,8,8,1]{3,4,2,1,0:T(2,128)(2,1)S(1)} %copy.54, bf16[7,8,64,8,72]{4,3,2,0,1:T(8,128)(2,1)} %reshape.389), kind=kOutput, calls=%fused_computation.9 | convolution fusion | flops 4128768 | bytes 5218304 | tf_op jit(solution)/shard_map/cshfg,cgshe->cfshe/dot_general | solution.py:22
  267.1 1.7 convert_element_type.106
  270.3 3.5 %fusion.8 = bf16[448,1152]{1,0:T(8,128)(2,1)} fusion(bf16[448,576]{1,0:T(8,128)(2,1)} %reshape.343, bf16[576,1152]{1,0:T(8,128)(2,1)} %param.12, bf16[448,1152]{1,0:T(8,128)(2,1)S(1)} %copy-done.6), kind=kOutput, calls=%fused_computation.17 | convolution fusion | flops 596090880 | bytes 3907584 | tf_op jit(solution)/shard_map/dot_general | solution.py:97
  (68 shorter events, 15.2 us)
Async XLA Ops:
  6.5 100.0 %copy-start = (bf16[576,1152]{1,0:T(8,128)(2,1)S(1)}, bf16[576,1152]{1,0:T(8,128)(2,1)}, u32[]{:S(2)}) copy-start(bf16[576,1152]{1,0:T(8,128)(2,1)} %param.10) | copy-start | bytes 3981316
  15.0 8.8 %copy-start.9 = (s32[224]{0:T(256)S(1)}, s32[224]{0:T(256)}, u32[]{:S(2)}) copy-start(s32[224]{0:T(256)} %param.15) | copy-start | bytes 2692
  15.0 10.1 %copy-start.2 = (s32[224]{0:T(256)S(1)}, s32[224]{0:T(256)}, u32[]{:S(2)}) copy-start(s32[224]{0:T(256)} %param.13) | copy-start | bytes 2692
  15.0 67.2 %all-to-all-start = ((bf16[32,1,64,1152]{3,2,1,0:T(8,128)(2,1)}), bf16[32,1,64,1152]{3,2,1,0:T(8,128)(2,1)}, u32[]{:S(2)}, u32[]{:S(2)}) async-start(bf16[32,1,64,1152]{3,2,1,0:T(8,128)(2,1)} %copy.38), calls=%async_computation | async-start | bytes 9437184 | tf_op jit(solution)/shard_map/all_to_all | solution.py:115
  23.8 161.2 %all-gather.7.cloned.1.call-start = ((), (), s32[]{:S(2)}) async-start(), calls=%async_computation.2 | async-start | bytes 5160960 | tf_op jit(solution)/shard_map/all_gather | solution.py:88
  86.5 1.0 copy-start.7
  104.4 2.1 copy-start.8
  106.6 3.3 %copy-start.10 = (bf16[1152,1728]{0,1:T(8,128)(2,1)S(1)}, bf16[1152,1728]{0,1:T(8,128)(2,1)}, u32[]{:S(2)}) copy-start(bf16[1152,1728]{0,1:T(8,128)(2,1)} %param.11) | copy-start | bytes 11943940
  108.9 1.0 copy-start.5
  122.4 1.9 copy-start.3
  123.3 120.5 %all-gather.5.cloned.1.call-start = ((), (), s32[]{:S(2)}) async-start(), calls=%async_computation.1 | async-start | bytes 5160960 | tf_op jit(solution)/shard_map/all_gather | solution.py:89
  129.1 68.4 %copy-start.4 = (bf16[7,64,8,72,1]{3,4,2,1,0:T(2,128)(2,1)S(1)}, bf16[7,64,8,72,1]{3,4,2,1,0:T(2,128)(2,1)}, u32[]{:S(2)}) copy-start(bf16[7,64,8,72,1]{3,4,2,1,0:T(2,128)(2,1)} %reshape.391) | copy-start | bytes 1548292
  267.1 3.2 %copy-start.6 = (bf16[448,1152]{1,0:T(8,128)(2,1)S(1)}, bf16[448,1152]{1,0:T(8,128)(2,1)}, u32[]{:S(2)}) copy-start(bf16[448,1152]{1,0:T(8,128)(2,1)} %copy-done.5) | copy-start | bytes 3096580
  268.8 5.0 %copy-start.1 = (bf16[576,1152]{1,0:T(8,128)(2,1)S(1)}, bf16[576,1152]{1,0:T(8,128)(2,1)}, u32[]{:S(2)}) copy-start(bf16[576,1152]{1,0:T(8,128)(2,1)} %param.10) | copy-start | bytes 3981316
Sparse Core Ops, SparseCore 0:
  123.5 61.4 all-gather.6
  186.7 57.0 all-gather.4
where the time goes:
time: 282 us; the launch traced here: 281 us
  waiting for transfers between devices  142 us (50%)
  local copies, waits for them, and re-layouts  68.4 us (24%)
  matrix products  41.7 us (15%)
  between operations  13.7 us (5%)
  starting transfers between devices  8.85 us (3%)
  other arithmetic  5.76 us (2%)
    all_to_all x1, waiting for transfers between devices, per_device(): lax.all_to_all(pack_out(select, latents), 'dp', split_axis=0, concat_axis...  56.4 us
    all_gather x1, waiting for transfers between devices, temporal_part(): lax.all_gather(qkv[:, :, :, 1], 'seq', axis=1, tiled=True)  55.8 us
    all_gather x1, waiting for transfers between devices, temporal_part(): lax.all_gather(qkv[:, :, :, 2], 'seq', axis=1, tiled=True)  30 us
    dot_general x2, matrix products, attend(): jnp.einsum(out_form, probs, values, preferred_element_type=jnp.float32)  12.6 us
    reshape x1, local copies, waits for them, and re-layouts, temporal_part(): values = values.reshape(count, total, slots, HEADS, HD)  12.5 us
    reshape x1, local copies, waits for them, and re-layouts, temporal_part(): keys = keys.reshape(count, total, slots, HEADS, HD)  12.5 us
    dot_general x1, matrix products, attend(): jnp.einsum(scores_form, query, keys, preferred_element_type=jnp.float32)  10.2 us
    all_to_all x1, starting transfers between devices, per_device(): lax.all_to_all(pack_out(select, latents), 'dp', split_axis=0, concat_axis...  8.77 us
  transfers between devices with their start and end apart: 3, of which 3 were waited for; matrix products, arithmetic and copies ran while one was open for 13% of the time, Pallas kernels for 0%

commit v1 on v0

v1 whole, which is shorter than its diff:
```python
import functools

import jax
import jax.numpy as jnp
from jax import lax
from jax.experimental import pallas as pl
from jax.experimental.pallas import tpu as pltpu
from jax.sharding import PartitionSpec as P

HEADS = 8
HD = 72
HW = 576
BLOCK = 128
VMEM = 51 * 1024 * 1024
ROWS_BY_ROWS = (((1,), (1,)), ((), ()))
COLUMNS_BY_COLUMNS = (((0,), (0,)), ((), ()))
SCALE = HD ** (-0.5) * 1.4426950408889634


def layer_norm(values):
    wide = values.astype(jnp.float32)
    centre = wide - jnp.mean(wide, axis=-1, keepdims=True)
    spread = jnp.mean(centre * centre, axis=-1, keepdims=True)
    return (centre * lax.rsqrt(spread + 1e-06)).astype(jnp.bfloat16)


def dot(left, right, dims):
    return lax.dot_general(left, right, dims, preferred_element_type=jnp.float32)


def attention_part(rows, w_q, w_k, w_v, w_out, biases):
    normed = layer_norm(rows)
    query = dot(w_q(), normed, ROWS_BY_ROWS)
    keys = dot(w_k(), normed, ROWS_BY_ROWS)
    probs = []
    start = 0
    for bias in biases:
        stop = start + bias.shape[0]
        for at in range(0, HW, HD):
            scores = dot(
                keys[at : at + HD, start:stop].astype(jnp.bfloat16),
                query[at : at + HD, start:stop].astype(jnp.bfloat16),
                COLUMNS_BY_COLUMNS,
            )
            scores = scores * SCALE + bias
            weight = jnp.exp2(scores - jnp.max(scores, axis=0, keepdims=True))
            total = jnp.sum(weight, axis=0, keepdims=True)
            probs.append((weight.astype(jnp.bfloat16), 1.0 / total))
        start = stop
    values = dot(w_v(), normed, ROWS_BY_ROWS)
    attn = []
    start = 0
    for index, bias in enumerate(biases):
        stop = start + bias.shape[0]
        heads = []
        for head in range(HEADS):
            at = head * HD
            weight, share = probs[index * HEADS + head]
            part = values[at : at + HD, start:stop].astype(jnp.bfloat16)
            heads.append(jnp.dot(part, weight, preferred_element_type=jnp.float32) * share)
        attn.append(jnp.concatenate(heads, axis=0))
        start = stop
    attn = jnp.concatenate(attn, axis=1).astype(jnp.bfloat16)
    block = rows.astype(jnp.float32) + dot(attn, w_out(), COLUMNS_BY_COLUMNS)
    return block.astype(jnp.bfloat16)


def iotas(size):
    return (
        lax.broadcasted_iota(jnp.int32, (size, size), 0),
        lax.broadcasted_iota(jnp.int32, (size, size), 1),
    )


def streamed(w_qkv, w_out, proj, back, sems):
    copies = [
        pltpu.make_async_copy(w_qkv.at[pl.ds(part * HW, HW)], proj.at[part], sems.at[part])
        for part in range(3)
    ]
    copies.append(pltpu.make_async_copy(w_out, back, sems.at[3]))
    for copy in copies:
        copy.start()

    def reader(part):
        def read():
            copies[part].wait()
            return proj[part] if part < 3 else back[...]

        return read

    return [reader(part) for part in range(4)]


def spatial_kernel(clips, slots, slen, x, w_qkv, w_out, out, proj, back, sems):
    weights = streamed(w_qkv, w_out, proj, back, sems)
    group = lax.axis_index("dp")
    total = clips * slots
    biases = []
    for start in range(0, total, BLOCK):
        size = min(BLOCK, total - start)
        row, col = iotas(size)
        live = jnp.zeros((size, size), jnp.bool_)
        for clip in range(start // slots, (start + size) // slots):
            first = clip * slots - start
            live = live | (
                (col >= first)
                & (col < first + slots)
                & (row >= first)
                & (row < first + slen[group * clips + clip])
            )
        biases.append(jnp.where(live, 0.0, -1e30))
    out[:total] = attention_part(x[...], *weights, biases)
    out[total:] = jnp.zeros((out.shape[0] - total, out.shape[1]), jnp.bfloat16)


def temporal_kernel(
    clips, slots, groups, frames, each, flen, target, x, w_qkv, w_out, out, proj, back, sems
):
    weights = streamed(w_qkv, w_out, proj, back, sems)
    home = lax.axis_index("dp") * frames + lax.axis_index("seq")
    slot = jnp.minimum(home * each // slots, clips - 1)
    span = frames * each
    total = groups * span
    row, col = iotas(BLOCK)
    same = (row // span == col // span) & (row % each == col % each)
    frame = row % span // each
    owner = row // span
    biases = []
    for start in range(0, total, BLOCK):
        most = jnp.zeros((BLOCK, BLOCK), jnp.int32)
        for part in range(BLOCK // span):
            group = start // span + part
            most = jnp.where(owner == part, flen[group * clips + slot], most)
        biases.append(jnp.where(same & (frame < most), 0.0, -1e30))
    block = attention_part(x[...], *weights, biases)
    for group in range(groups):
        goal = target[group * clips + slot] // clips
        out[pl.ds(pl.multiple_of(goal * span, span), span), :] = block[
            group * span : (group + 1) * span
        ]


def per_device(
    latents,
    w_spatial_qkv,
    w_spatial_out,
    w_temporal_qkv,
    w_temporal_out,
    spatial_len,
    frames_len,
    target,
):
    clips, _, slots, width = latents.shape
    groups, frames = lax.axis_size("dp"), lax.axis_size("seq")
    devices = groups * frames
    each = -(-clips * slots // devices)
    rows = devices * each
    smem = pl.BlockSpec(memory_space=pltpu.SMEM)
    vmem = pl.BlockSpec(memory_space=pltpu.VMEM)
    hbm = pl.BlockSpec(memory_space=pl.ANY)

    def exchange(values):
        return lax.all_to_all(
            values.reshape(devices, each, width),
            ("dp", "seq"),
            split_axis=0,
            concat_axis=0,
            tiled=True,
        ).reshape(rows, width)

    def call(kernel, scalars, values, w_qkv, w_out):
        return pl.pallas_call(
            kernel,
            out_shape=jax.ShapeDtypeStruct((rows, width), jnp.bfloat16),
            in_specs=[smem] * len(scalars) + [vmem, hbm, hbm],
            out_specs=vmem,
            scratch_shapes=[
                pltpu.VMEM((3, HW, width), jnp.bfloat16),
                pltpu.VMEM((HW, width), jnp.bfloat16),
                pltpu.SemaphoreType.DMA((4,)),
            ],
            compiler_params=pltpu.CompilerParams(vmem_limit_bytes=VMEM),
        )(*scalars, values, w_qkv.T, w_out)

    mid = call(
        functools.partial(spatial_kernel, clips, slots),
        [spatial_len],
        latents.reshape(clips * slots, width),
        w_spatial_qkv,
        w_spatial_out,
    )
    block = call(
        functools.partial(temporal_kernel, clips, slots, groups, frames, each),
        [frames_len, target],
        exchange(mid),
        w_temporal_qkv,
        w_temporal_out,
    )
    return exchange(block)[: clips * slots].reshape(latents.shape)


def solution(mesh):
    return jax.shard_map(
        per_device,
        mesh=mesh,
        in_specs=(P("dp", "seq", None, None), P(), P(), P(), P(), P(), P(), P()),
        out_specs=P("dp", "seq", None, None),
        check_vma=False,
    )
```

time: 282 us -> 111 us (0.39)
  waiting for transfers between devices: 142 us -> 0 us
  blocking collectives: 0 us -> 90.9 us
  local copies, waits for them, and re-layouts: 68.4 us -> 5.63 us
  matrix products: 41.7 us -> 0 us
  Pallas kernels: 0 us -> 14.3 us
  between operations: 13.7 us -> 0.05 us
  starting transfers between devices: 8.85 us -> 0 us
  other arithmetic: 5.76 us -> 0 us
    all_to_all x0 -> x2, blocking collectives: none -> 90.9 us  [exchange(): lax.all_to_all(values.reshape(devices, each, width), ('dp', 'seq'), split...]
    all_gather x2 -> x0, waiting for transfers between devices: 85.8 us -> none  [the longest x1 55.8 us: temporal_part(): lax.all_gather(qkv[:, :, :, 1], 'seq', axis=1, tiled=True)]
    all_to_all x1 -> x0, waiting for transfers between devices: 56.4 us -> none  [per_device(): lax.all_to_all(pack_out(select, latents), 'dp', split_axis=0, concat_axis...]
    dot_general x8 -> x0, matrix products: 38.3 us -> none  [the longest x2 12.6 us: attend(): jnp.einsum(out_form, probs, values, preferred_element_type=jnp.float32)]
    reshape x6 -> x4, local copies, waits for them, and re-layouts: 34.7 us -> 2.79 us  [the longest x1 1.35 us: per_device(): return exchange(block)[:clips * slots].reshape(latents.shape)]
    pallas_call x0 -> x2, Pallas kernels: none -> 14.3 us  [call(): pl.pallas_call(kernel, out_shape=jax.ShapeDtypeStruct((rows, width), jnp....]
    slice x4 -> x1, local copies, waits for them, and re-layouts: 12.3 us -> 0.71 us  [per_device(): return exchange(block)[:clips * slots].reshape(latents.shape)]
    all_to_all x1 -> x0, starting transfers between devices: 8.77 us -> none  [per_device(): lax.all_to_all(pack_out(select, latents), 'dp', split_axis=0, concat_axis...]
  transfers between devices with their start and end apart: 3 -> 0, of which waited for: 3 -> 0; matrix products, arithmetic and copies ran while one was open for 13% -> 0% of each run, Pallas kernels for 0% -> 0%
where the time goes in v1:
time: 111 us
  blocking collectives  90.9 us (82%)
  Pallas kernels  14.3 us (13%)
  local copies, waits for them, and re-layouts  5.63 us (5%)
    all_to_all x2, blocking collectives, exchange(): lax.all_to_all(values.reshape(devices, each, width), ('dp', 'seq'), split...  90.9 us
    pallas_call x2, Pallas kernels, call(): pl.pallas_call(kernel, out_shape=jax.ShapeDtypeStruct((rows, width), jnp....  14.3 us

profile of v1, /device:TPU:1, one launch (start us, length us, event | category | flops | bytes accessed | tf_op | source)
XLA Modules:
  0.0 110.9 jit_solution(1027625260048858400)
XLA Ops:
  0.0 0.0 copy-start
  0.0 1.2 %copy-done = bf16[7,1,64,1152]{3,2,1,0:T(8,128)(2,1)S(1)} copy-done((bf16[7,1,64,1152]{3,2,1,0:T(8,128)(2,1)S(1)}, bf16[7,1,64,1152]{3,2,1,0:T(8,128)(2,1)}, u32[]{:S(2)}) %copy-start) | copy-done | bytes 1032216
  1.2 0.0 copy-start.3
  1.2 0.7 copy-done.3
  1.9 6.9 %shard_map.82 = bf16[512,1152]{1,0:T(8,128)(2,1)S(1)} custom-call(s32[224]{0:T(256)S(1)} %copy-done.3, bf16[448,1152]{1,0:T(8,128)(2,1)S(1)} %bitcast.3, bf16[1728,1152]{1,0:T(8,128)(2,1)} %bitcast.4, bf16[576,1152]{1,0:T(8,128)(2,1)} %w_out.2), custom_call_target="tpu_custom_call" | custom-call | tf_op jit(solution)/shard_map/pallas_call | solution.py:172
  8.9 0.5 reshape.19
  9.4 50.3 %all_to_all.10 = bf16[256,2,1152]{2,1,0:T(2,128)(2,1)S(1)} all-to-all(bf16[256,2,1152]{2,1,0:T(2,128)(2,1)S(1)} %reshape.19), channel_id=1, replica_groups=mesh['dp'=32,'seq'=8] {'dp','seq'}, dimensions={0} | all-to-all | bytes 2359296 | tf_op jit(solution)/shard_map/all_to_all | solution.py:163
  59.6 0.0 copy-start.1
  59.6 0.0 copy-start.2
  59.6 0.5 reshape.20.x
  60.1 0.2 copy-done.1
  60.3 0.0 copy-done.2
  60.3 7.4 %shard_map.83 = bf16[512,1152]{1,0:T(8,128)(2,1)S(1)} custom-call(s32[224]{0:T(256)S(1)} %copy-done.1, s32[224]{0:T(256)S(1)} %copy-done.2, bf16[512,1152]{1,0:T(8,128)(2,1)S(1)} %reshape.20.x, bf16[1728,1152]{1,0:T(8,128)(2,1)} %bitcast.5, bf16[576,1152]{1,0:T(8,128)(2,1)} %w_out.3), custom_call_target="tpu_custom_call" | custom-call | tf_op jit(solution)/shard_map/pallas_call | solution.py:172
  67.7 0.5 reshape.21
  68.2 40.6 %all_to_all.11 = bf16[256,2,1152]{2,1,0:T(2,128)(2,1)S(1)} all-to-all(bf16[256,2,1152]{2,1,0:T(2,128)(2,1)S(1)} %reshape.21), channel_id=1, replica_groups=mesh['dp'=32,'seq'=8] {'dp','seq'}, dimensions={0} | all-to-all | bytes 2359296 | tf_op jit(solution)/shard_map/all_to_all | solution.py:163
  108.9 0.7 slice.5
  109.6 1.3 %reshape.22 = bf16[7,1,64,1152]{3,2,1,0:T(8,128)(2,1)} reshape(bf16[224,2,1152]{2,1,0:T(2,128)(2,1)S(1)} %slice.5) | data formatting | bytes 2064384 | tf_op jit(solution)/shard_map/reshape | solution.py:199
Async XLA Ops:
  0.0 1.2 %copy-start = (bf16[7,1,64,1152]{3,2,1,0:T(8,128)(2,1)S(1)}, bf16[7,1,64,1152]{3,2,1,0:T(8,128)(2,1)}, u32[]{:S(2)}) copy-start(bf16[7,1,64,1152]{3,2,1,0:T(8,128)(2,1)} %param.8) | copy-start | bytes 3096580
  1.2 0.7 copy-start.3
  59.6 0.7 copy-start.1
  59.6 0.7 copy-start.2

commit v2 on v1

--- a/solution.py
+++ b/solution.py
@@ -11,7 +11,7 @@
 HD = 72
 HW = 576
 BLOCK = 128
-VMEM = 51 * 1024 * 1024
+MIB = 1024 * 1024
 ROWS_BY_ROWS = (((1,), (1,)), ((), ()))
 COLUMNS_BY_COLUMNS = (((0,), (0,)), ((), ()))
 SCALE = HD ** (-0.5) * 1.4426950408889634
@@ -78,8 +78,6 @@
         for part in range(3)
     ]
     copies.append(pltpu.make_async_copy(w_out, back, sems.at[3]))
-    for copy in copies:
-        copy.start()
 
     def reader(part):
         def read():
@@ -88,11 +86,14 @@
 
         return read
 
-    return [reader(part) for part in range(4)]
-
-
-def spatial_kernel(clips, slots, slen, x, w_qkv, w_out, out, proj, back, sems):
-    weights = streamed(w_qkv, w_out, proj, back, sems)
+    return copies, [reader(part) for part in range(4)]
+
+
+def spatial_kernel(clips, slots, slen, x, w_qkv, w_out, out, proj, back, sems, own):
+    copies, weights = streamed(w_qkv, w_out, proj, back, sems)
+    arrival = pltpu.make_async_copy(x, own, sems.at[4])
+    arrival.start()
+    copies[0].start()
     group = lax.axis_index("dp")
     total = clips * slots
     biases = []
@@ -109,35 +110,68 @@
                 & (row < first + slen[group * clips + clip])
             )
         biases.append(jnp.where(live, 0.0, -1e30))
-    out[:total] = attention_part(x[...], *weights, biases)
     out[total:] = jnp.zeros((out.shape[0] - total, out.shape[1]), jnp.bfloat16)
+    arrival.wait()
+    for copy in copies[1:]:
+        copy.start()
+    out[:total] = attention_part(own[...], *weights, biases)
 
 
 def temporal_kernel(
     clips, slots, groups, frames, each, flen, target, x, w_qkv, w_out, out, proj, back, sems
 ):
-    weights = streamed(w_qkv, w_out, proj, back, sems)
-    home = lax.axis_index("dp") * frames + lax.axis_index("seq")
+    copies, weights = streamed(w_qkv, w_out, proj, back, sems)
+    for copy in copies:
+        copy.start()
+    home = lax.axis_index("seq") * groups + lax.axis_index("dp")
     slot = jnp.minimum(home * each // slots, clips - 1)
-    span = frames * each
-    total = groups * span
+    plane = groups * each
+    row, col = iotas(plane)
+    goal = jnp.zeros((plane, plane), jnp.int32)
+    most = jnp.zeros((plane, plane), jnp.int32)
+    for group in range(groups):
+        here = col // each == group
+        goal = jnp.where(here, target[group * clips + slot] // clips, goal)
+        most = jnp.where(here, flen[group * clips + slot], most)
+    moved = (goal == row // each) & (row % each == col % each)
+    most = jnp.sum(jnp.where(moved, most.astype(jnp.float32), 0.0), axis=1, keepdims=True)
+    moved = jnp.where(moved, 1.0, 0.0).astype(jnp.bfloat16)
+    planes = [
+        jnp.dot(
+            moved, x[frame * plane : (frame + 1) * plane], preferred_element_type=jnp.float32
+        ).astype(jnp.bfloat16)
+        for frame in range(frames)
+    ]
+    part = BLOCK // frames
+    starts = range(0, plane, part)
     row, col = iotas(BLOCK)
-    same = (row // span == col // span) & (row % each == col % each)
-    frame = row % span // each
-    owner = row // span
+    same = row % part == col % part
+    frame = (row // part).astype(jnp.float32)
     biases = []
-    for start in range(0, total, BLOCK):
-        most = jnp.zeros((BLOCK, BLOCK), jnp.int32)
-        for part in range(BLOCK // span):
-            group = start // span + part
-            most = jnp.where(owner == part, flen[group * clips + slot], most)
-        biases.append(jnp.where(same & (frame < most), 0.0, -1e30))
-    block = attention_part(x[...], *weights, biases)
-    for group in range(groups):
-        goal = target[group * clips + slot] // clips
-        out[pl.ds(pl.multiple_of(goal * span, span), span), :] = block[
-            group * span : (group + 1) * span
-        ]
+    for start in starts:
+        live = jnp.concatenate([most[start : start + part]] * frames, axis=0)
+        biases.append(jnp.where(same & (frame < live), 0.0, -1e30))
+    rows = jnp.concatenate([each[start : start + part] for start in starts for each in planes])
+    block = attention_part(rows, *weights, biases)
+    for index, start in enumerate(starts):
+        for frame in range(frames):
+            at = frame * plane + start
+            first = index * BLOCK + frame * part
+            out[at : at + part] = block[first : first + part]
+
+
+def crop_kernel(pieces, x, out, sems):
+    size = out.shape[0] // pieces
+    copies = [
+        pltpu.make_async_copy(
+            x.at[pl.ds(piece * size, size)], out.at[pl.ds(piece * size, size)], sems.at[piece]
+        )
+        for piece in range(pieces)
+    ]
+    for copy in copies:
+        copy.start()
+    for copy in copies:
+        copy.wait()
 
 
 def per_device(
@@ -162,24 +196,25 @@
     def exchange(values):
         return lax.all_to_all(
             values.reshape(devices, each, width),
-            ("dp", "seq"),
+            ("seq", "dp"),
             split_axis=0,
             concat_axis=0,
             tiled=True,
         ).reshape(rows, width)
 
-    def call(kernel, scalars, values, w_qkv, w_out):
+    def call(kernel, scalars, values, w_qkv, w_out, where, limit, extra):
         return pl.pallas_call(
             kernel,
-            out_shape=jax.ShapeDtypeStruct((rows, width), jnp.bfloat16),
-            in_specs=[smem] * len(scalars) + [vmem, hbm, hbm],
+            out_shape=pltpu.VMEM((rows, width), jnp.bfloat16),
+            in_specs=[smem] * len(scalars) + [where, hbm, hbm],
             out_specs=vmem,
             scratch_shapes=[
                 pltpu.VMEM((3, HW, width), jnp.bfloat16),
                 pltpu.VMEM((HW, width), jnp.bfloat16),
-                pltpu.SemaphoreType.DMA((4,)),
+                pltpu.SemaphoreType.DMA((5,)),
+                *extra,
             ],
-            compiler_params=pltpu.CompilerParams(vmem_limit_bytes=VMEM),
+            compiler_params=pltpu.CompilerParams(vmem_limit_bytes=limit),
         )(*scalars, values, w_qkv.T, w_out)
 
     mid = call(
@@ -188,6 +223,9 @@
         latents.reshape(clips * slots, width),
         w_spatial_qkv,
         w_spatial_out,
+        hbm,
+        55 * MIB,
+        [pltpu.VMEM((clips * slots, width), jnp.bfloat16)],
     )
     block = call(
         functools.partial(temporal_kernel, clips, slots, groups, frames, each),
@@ -195,8 +233,19 @@
         exchange(mid),
         w_temporal_qkv,
         w_temporal_out,
-    )
-    return exchange(block)[: clips * slots].reshape(latents.shape)
+        vmem,
+        51 * MIB,
+        [],
+    )
+    final = pl.pallas_call(
+        functools.partial(crop_kernel, clips),
+        out_shape=jax.ShapeDtypeStruct((clips * slots, width), jnp.bfloat16),
+        in_specs=[hbm],
+        out_specs=hbm,
+        scratch_shapes=[pltpu.SemaphoreType.DMA((clips,))],
+        compiler_params=pltpu.CompilerParams(vmem_limit_bytes=40 * MIB),
+    )(exchange(block))
+    return final.reshape(latents.shape)
 
 
 def solution(mesh):

time: 111 us -> 107 us (0.964)
  local copies, waits for them, and re-layouts: 5.63 us -> 2.14 us
  blocking collectives: 90.9 us -> 88.4 us
  Pallas kernels: 14.3 us -> 15.8 us
    all_to_all x2, blocking collectives: 90.9 us -> 88.4 us  [exchange(): lax.all_to_all(values.reshape(devices, each, width), ('seq', 'dp'), split...]
    unnamed x8 -> x4, local copies, waits for them, and re-layouts: 2.12 us -> 0.23 us
    pallas_call x2 -> x3, Pallas kernels: 14.3 us -> 15.8 us  [the longest x2 14.8 us: call(): pl.pallas_call(kernel, out_shape=pltpu.VMEM((rows, width), jnp.bfloat16),...]
where the time goes in v2:
time: 107 us; the launch traced here: 106 us
  blocking collectives  88.4 us (83%)
  Pallas kernels  15.8 us (15%)
  local copies, waits for them, and re-layouts  2.14 us (2%)
    all_to_all x2, blocking collectives, exchange(): lax.all_to_all(values.reshape(devices, each, width), ('seq', 'dp'), split...  88.4 us
    pallas_call x2, Pallas kernels, call(): pl.pallas_call(kernel, out_shape=pltpu.VMEM((rows, width), jnp.bfloat16),...  14.8 us

profile of v2, /device:TPU:1, one launch (start us, length us, event | category | flops | bytes accessed | tf_op | source)
XLA Modules:
  0.0 106.4 jit_solution(7292253359010451647)
XLA Ops:
  0.0 7.4 %shard_map.82 = bf16[512,1152]{1,0:T(8,128)(2,1)S(1)} custom-call(s32[224]{0:T(256)} %slen.1, bf16[448,1152]{1,0:T(8,128)(2,1)} %bitcast.8, bf16[1728,1152]{1,0:T(8,128)(2,1)} %bitcast.6, bf16[576,1152]{1,0:T(8,128)(2,1)} %w_out.2), custom_call_target="tpu_custom_call" | custom-call | tf_op jit(solution)/shard_map/pallas_call | solution.py:206
  7.4 0.5 reshape.19
  7.9 48.7 %all_to_all.10 = bf16[256,2,1152]{2,1,0:T(2,128)(2,1)S(1)} all-to-all(bf16[256,2,1152]{2,1,0:T(2,128)(2,1)S(1)} %reshape.19), channel_id=1, replica_groups=mesh['dp'=32,'seq'=8] {'seq','dp'}, dimensions={0} | all-to-all | bytes 2359296 | tf_op jit(solution)/shard_map/all_to_all | solution.py:197
  56.6 0.0 copy-start
  56.6 0.0 copy-start.1
  56.6 0.5 reshape.20.x
  57.1 0.2 copy-done
  57.3 0.0 copy-done.1
  57.3 7.4 %shard_map.83 = bf16[512,1152]{1,0:T(8,128)(2,1)S(1)} custom-call(s32[224]{0:T(256)S(1)} %copy-done, s32[224]{0:T(256)S(1)} %copy-done.1, bf16[512,1152]{1,0:T(8,128)(2,1)S(1)} %reshape.20.x, bf16[1728,1152]{1,0:T(8,128)(2,1)} %bitcast.7, bf16[576,1152]{1,0:T(8,128)(2,1)} %w_out.3), custom_call_target="tpu_custom_call" | custom-call | tf_op jit(solution)/shard_map/pallas_call | solution.py:206
  64.8 0.5 reshape.21
  65.3 39.6 %all_to_all.11 = bf16[256,2,1152]{2,1,0:T(2,128)(2,1)S(1)} all-to-all(bf16[256,2,1152]{2,1,0:T(2,128)(2,1)S(1)} %reshape.21), channel_id=1, replica_groups=mesh['dp'=32,'seq'=8] {'seq','dp'}, dimensions={0} | all-to-all | bytes 2359296 | tf_op jit(solution)/shard_map/all_to_all | solution.py:197
  104.9 0.5 reshape.22.x
  105.4 1.0 shard_map.84
Async XLA Ops:
  56.6 0.7 copy-start
  56.6 0.7 copy-start.1

commit v3 on v2

--- a/solution.py
+++ b/solution.py
@@ -81,7 +81,8 @@
 
     def reader(part):
         def read():
-            copies[part].wait()
+            for copy in {0: copies[:1], 1: copies[1:]}.get(part, []):
+                copy.wait()
             return proj[part] if part < 3 else back[...]
 
         return read

time: 107 us -> 107 us (level)
  no operation moved by 1% of the time
where the time goes in v3:
time: 107 us; the launch traced here: 106 us
  blocking collectives  88.4 us (83%)
  Pallas kernels  15.8 us (15%)
  local copies, waits for them, and re-layouts  2.14 us (2%)
    all_to_all x2, blocking collectives, exchange(): lax.all_to_all(values.reshape(devices, each, width), ('seq', 'dp'), split...  88.4 us
    pallas_call x2, Pallas kernels, call(): pl.pallas_call(kernel, out_shape=pltpu.VMEM((rows, width), jnp.bfloat16),...  14.7 us

profile of v3, /device:TPU:1, one launch (start us, length us, event | category | flops | bytes accessed | tf_op | source)
XLA Modules:
  0.0 106.3 jit_solution(10020073119284420868)
XLA Ops:
  0.0 7.6 %shard_map.82 = bf16[512,1152]{1,0:T(8,128)(2,1)S(1)} custom-call(s32[224]{0:T(256)} %slen.1, bf16[448,1152]{1,0:T(8,128)(2,1)} %bitcast.8, bf16[1728,1152]{1,0:T(8,128)(2,1)} %bitcast.6, bf16[576,1152]{1,0:T(8,128)(2,1)} %w_out.2), custom_call_target="tpu_custom_call" | custom-call | tf_op jit(solution)/shard_map/pallas_call | solution.py:207
  7.6 0.5 reshape.19
  8.1 48.7 %all_to_all.10 = bf16[256,2,1152]{2,1,0:T(2,128)(2,1)S(1)} all-to-all(bf16[256,2,1152]{2,1,0:T(2,128)(2,1)S(1)} %reshape.19), channel_id=1, replica_groups=mesh['dp'=32,'seq'=8] {'seq','dp'}, dimensions={0} | all-to-all | bytes 2359296 | tf_op jit(solution)/shard_map/all_to_all | solution.py:198
  56.9 0.0 copy-start
  56.9 0.0 copy-start.1
  56.9 0.5 reshape.20.x
  57.4 0.2 copy-done
  57.6 0.0 copy-done.1
  57.6 7.1 %shard_map.83 = bf16[512,1152]{1,0:T(8,128)(2,1)S(1)} custom-call(s32[224]{0:T(256)S(1)} %copy-done, s32[224]{0:T(256)S(1)} %copy-done.1, bf16[512,1152]{1,0:T(8,128)(2,1)S(1)} %reshape.20.x, bf16[1728,1152]{1,0:T(8,128)(2,1)} %bitcast.7, bf16[576,1152]{1,0:T(8,128)(2,1)} %w_out.3), custom_call_target="tpu_custom_call" | custom-call | tf_op jit(solution)/shard_map/pallas_call | solution.py:207
  64.7 0.5 reshape.21
  65.2 39.7 %all_to_all.11 = bf16[256,2,1152]{2,1,0:T(2,128)(2,1)S(1)} all-to-all(bf16[256,2,1152]{2,1,0:T(2,128)(2,1)S(1)} %reshape.21), channel_id=1, replica_groups=mesh['dp'=32,'seq'=8] {'seq','dp'}, dimensions={0} | all-to-all | bytes 2359296 | tf_op jit(solution)/shard_map/all_to_all | solution.py:198
  104.8 0.5 reshape.22.x
  105.3 1.0 shard_map.84
Async XLA Ops:
  56.9 0.7 copy-start
  56.9 0.7 copy-start.1

commit v4 on v3

--- a/solution.py
+++ b/solution.py
@@ -111,11 +111,14 @@
                 & (row < first + slen[group * clips + clip])
             )
         biases.append(jnp.where(live, 0.0, -1e30))
-    out[total:] = jnp.zeros((out.shape[0] - total, out.shape[1]), jnp.bfloat16)
+    each, width = out.shape[1:]
+    filled = total // each
+    out[filled:] = jnp.zeros((out.shape[0] - filled, each, width), jnp.bfloat16)
     arrival.wait()
     for copy in copies[1:]:
         copy.start()
-    out[:total] = attention_part(own[...], *weights, biases)
+    block = attention_part(own[...], *weights, biases)
+    out[:filled] = block.reshape(filled, each, width)
 
 
 def temporal_kernel(
@@ -139,7 +142,9 @@
     moved = jnp.where(moved, 1.0, 0.0).astype(jnp.bfloat16)
     planes = [
         jnp.dot(
-            moved, x[frame * plane : (frame + 1) * plane], preferred_element_type=jnp.float32
+            moved,
+            x[frame * groups : (frame + 1) * groups].reshape(plane, x.shape[2]),
+            preferred_element_type=jnp.float32,
         ).astype(jnp.bfloat16)
         for frame in range(frames)
     ]
@@ -152,25 +157,28 @@
     for start in starts:
         live = jnp.concatenate([most[start : start + part]] * frames, axis=0)
         biases.append(jnp.where(same & (frame < live), 0.0, -1e30))
-    rows = jnp.concatenate([each[start : start + part] for start in starts for each in planes])
+    rows = jnp.concatenate([held[start : start + part] for start in starts for held in planes])
     block = attention_part(rows, *weights, biases)
     for index, start in enumerate(starts):
         for frame in range(frames):
-            at = frame * plane + start
+            at = (frame * plane + start) // each
             first = index * BLOCK + frame * part
-            out[at : at + part] = block[first : first + part]
-
-
-def crop_kernel(pieces, x, out, sems):
-    size = out.shape[0] // pieces
-    copies = [
-        pltpu.make_async_copy(
-            x.at[pl.ds(piece * size, size)], out.at[pl.ds(piece * size, size)], sems.at[piece]
+            out[at : at + part // each] = block[first : first + part].reshape(
+                part // each, each, block.shape[1]
+            )
+
+
+def crop_kernel(pieces, x, out, rows, sems):
+    size, width = out.shape[0] // pieces, out.shape[1]
+    chunk = size // x.shape[1]
+    copies = []
+    for piece in range(pieces):
+        span = pl.ds(piece * size, size)
+        rows[piece * size : (piece + 1) * size] = x[piece * chunk : (piece + 1) * chunk].reshape(
+            size, width
         )
-        for piece in range(pieces)
-    ]
-    for copy in copies:
-        copy.start()
+        copies.append(pltpu.make_async_copy(rows.at[span], out.at[span], sems.at[piece]))
+        copies[-1].start()
     for copy in copies:
         copy.wait()
 
@@ -189,24 +197,23 @@
     groups, frames = lax.axis_size("dp"), lax.axis_size("seq")
     devices = groups * frames
     each = -(-clips * slots // devices)
-    rows = devices * each
     smem = pl.BlockSpec(memory_space=pltpu.SMEM)
     vmem = pl.BlockSpec(memory_space=pltpu.VMEM)
     hbm = pl.BlockSpec(memory_space=pl.ANY)
 
     def exchange(values):
         return lax.all_to_all(
-            values.reshape(devices, each, width),
+            values,
             ("seq", "dp"),
             split_axis=0,
             concat_axis=0,
             tiled=True,
-        ).reshape(rows, width)
+        )
 
     def call(kernel, scalars, values, w_qkv, w_out, where, limit, extra):
         return pl.pallas_call(
             kernel,
-            out_shape=pltpu.VMEM((rows, width), jnp.bfloat16),
+            out_shape=pltpu.VMEM((devices, each, width), jnp.bfloat16),
             in_specs=[smem] * len(scalars) + [where, hbm, hbm],
             out_specs=vmem,
             scratch_shapes=[
@@ -241,9 +248,12 @@
     final = pl.pallas_call(
         functools.partial(crop_kernel, clips),
         out_shape=jax.ShapeDtypeStruct((clips * slots, width), jnp.bfloat16),
-        in_specs=[hbm],
+        in_specs=[vmem],
         out_specs=hbm,
-        scratch_shapes=[pltpu.SemaphoreType.DMA((clips,))],
+        scratch_shapes=[
+            pltpu.VMEM((clips * slots, width), jnp.bfloat16),
+            pltpu.SemaphoreType.DMA((clips,)),
+        ],
         compiler_params=pltpu.CompilerParams(vmem_limit_bytes=40 * MIB),
     )(exchange(block))
     return final.reshape(latents.shape)

time: 107 us -> 104 us (0.972)
  local copies, waits for them, and re-layouts: 2.14 us -> 0.01 us
    reshape x4 -> x0, local copies, waits for them, and re-layouts: 1.91 us -> none  [the longest x2 0.98 us: exchange(): values.reshape(devices, each, width)]
where the time goes in v4:
time: 104 us
  blocking collectives  88.4 us (85%)
  Pallas kernels  15.9 us (15%)
    all_to_all x2, blocking collectives, exchange(): lax.all_to_all(values, ('seq', 'dp'), split_axis=0, concat_axis=0, tiled=...  88.4 us
    pallas_call x2, Pallas kernels, call(): pl.pallas_call(kernel, out_shape=pltpu.VMEM((devices, each, width), jnp.b...  14.8 us

profile of v4, /device:TPU:1, one launch (start us, length us, event | category | flops | bytes accessed | tf_op | source)
XLA Modules:
  0.0 104.3 jit_solution(17064588896051387211)
XLA Ops:
  0.0 7.7 %shard_map.82 = bf16[256,2,1152]{2,1,0:T(2,128)(2,1)S(1)} custom-call(s32[224]{0:T(256)} %slen.1, bf16[448,1152]{1,0:T(8,128)(2,1)} %bitcast.8, bf16[1728,1152]{1,0:T(8,128)(2,1)} %bitcast.6, bf16[576,1152]{1,0:T(8,128)(2,1)} %w_out.2), custom_call_target="tpu_custom_call" | custom-call | tf_op jit(solution)/shard_map/pallas_call | solution.py:214
  7.7 0.0 copy-start
  7.7 0.0 copy-start.1
  7.7 48.7 %all_to_all.10.x = bf16[256,2,1152]{2,1,0:T(2,128)(2,1)S(1)} all-to-all(bf16[256,2,1152]{2,1,0:T(2,128)(2,1)S(1)} %shard_map.82), channel_id=1, replica_groups=mesh['dp'=32,'seq'=8] {'seq','dp'}, dimensions={0} | all-to-all | bytes 2359296 | tf_op jit(solution)/shard_map/all_to_all | solution.py:205
  56.5 0.0 copy-done
  56.5 0.0 copy-done.1
  56.5 7.1 %shard_map.83 = bf16[256,2,1152]{2,1,0:T(2,128)(2,1)S(1)} custom-call(s32[224]{0:T(256)S(1)} %copy-done, s32[224]{0:T(256)S(1)} %copy-done.1, bf16[256,2,1152]{2,1,0:T(2,128)(2,1)S(1)} %all_to_all.10.x, bf16[1728,1152]{1,0:T(8,128)(2,1)} %bitcast.7, bf16[576,1152]{1,0:T(8,128)(2,1)} %w_out.3), custom_call_target="tpu_custom_call" | custom-call | tf_op jit(solution)/shard_map/pallas_call | solution.py:214
  63.6 39.6 %all_to_all.11.x = bf16[256,2,1152]{2,1,0:T(2,128)(2,1)S(1)} all-to-all(bf16[256,2,1152]{2,1,0:T(2,128)(2,1)S(1)} %shard_map.83), channel_id=1, replica_groups=mesh['dp'=32,'seq'=8] {'seq','dp'}, dimensions={0} | all-to-all | bytes 2359296 | tf_op jit(solution)/shard_map/all_to_all | solution.py:205
  103.3 1.0 shard_map.84
Async XLA Ops:
  7.7 48.8 %copy-start = (s32[224]{0:T(256)S(1)}, s32[224]{0:T(256)}, u32[]{:S(2)}) copy-start(s32[224]{0:T(256)} %flen.1) | copy-start | bytes 2692
  7.7 48.7 %copy-start.1 = (s32[224]{0:T(256)S(1)}, s32[224]{0:T(256)}, u32[]{:S(2)}) copy-start(s32[224]{0:T(256)} %target.1) | copy-start | bytes 2692

commit v5 on v4

--- a/solution.py
+++ b/solution.py
@@ -90,7 +90,23 @@
     return copies, [reader(part) for part in range(4)]
 
 
-def spatial_kernel(clips, slots, slen, x, w_qkv, w_out, out, proj, back, sems, own):
+def spatial_kernel(
+    clips,
+    slots,
+    slen,
+    x,
+    w_qkv,
+    w_out,
+    next_qkv,
+    next_out,
+    out,
+    kept_qkv,
+    kept_out,
+    proj,
+    back,
+    sems,
+    own,
+):
     copies, weights = streamed(w_qkv, w_out, proj, back, sems)
     arrival = pltpu.make_async_copy(x, own, sems.at[4])
     arrival.start()
@@ -117,16 +133,26 @@
     arrival.wait()
     for copy in copies[1:]:
         copy.start()
-    block = attention_part(own[...], *weights, biases)
+    later = [
+        pltpu.make_async_copy(next_qkv, kept_qkv, sems.at[5]),
+        pltpu.make_async_copy(next_out, kept_out, sems.at[6]),
+    ]
+
+    def keys_weights():
+        held = weights[1]()
+        for copy in later:
+            copy.start()
+        return held
+
+    block = attention_part(own[...], weights[0], keys_weights, *weights[2:], biases)
     out[:filled] = block.reshape(filled, each, width)
+    for copy in later:
+        copy.wait()
 
 
 def temporal_kernel(
-    clips, slots, groups, frames, each, flen, target, x, w_qkv, w_out, out, proj, back, sems
+    clips, slots, groups, frames, each, flen, target, x, w_qkv, w_out, out
 ):
-    copies, weights = streamed(w_qkv, w_out, proj, back, sems)
-    for copy in copies:
-        copy.start()
     home = lax.axis_index("seq") * groups + lax.axis_index("dp")
     slot = jnp.minimum(home * each // slots, clips - 1)
     plane = groups * each
@@ -158,7 +184,14 @@
         live = jnp.concatenate([most[start : start + part]] * frames, axis=0)
         biases.append(jnp.where(same & (frame < live), 0.0, -1e30))
     rows = jnp.concatenate([held[start : start + part] for start in starts for held in planes])
-    block = attention_part(rows, *weights, biases)
+    block = attention_part(
+        rows,
+        lambda: w_qkv[:HW],
+        lambda: w_qkv[HW : 2 * HW],
+        lambda: w_qkv[2 * HW :],
+        lambda: w_out[...],
+        biases,
+    )
     for index, start in enumerate(starts):
         for frame in range(frames):
             at = (frame * plane + start) // each
@@ -210,41 +243,38 @@
             tiled=True,
         )
 
-    def call(kernel, scalars, values, w_qkv, w_out, where, limit, extra):
-        return pl.pallas_call(
-            kernel,
-            out_shape=pltpu.VMEM((devices, each, width), jnp.bfloat16),
-            in_specs=[smem] * len(scalars) + [where, hbm, hbm],
-            out_specs=vmem,
-            scratch_shapes=[
-                pltpu.VMEM((3, HW, width), jnp.bfloat16),
-                pltpu.VMEM((HW, width), jnp.bfloat16),
-                pltpu.SemaphoreType.DMA((5,)),
-                *extra,
-            ],
-            compiler_params=pltpu.CompilerParams(vmem_limit_bytes=limit),
-        )(*scalars, values, w_qkv.T, w_out)
-
-    mid = call(
+    shape = (devices, each, width)
+    mid, w_qkv, w_out = pl.pallas_call(
         functools.partial(spatial_kernel, clips, slots),
-        [spatial_len],
+        out_shape=[
+            pltpu.VMEM(shape, jnp.bfloat16),
+            pltpu.VMEM((3 * HW, width), jnp.bfloat16),
+            pltpu.VMEM((HW, width), jnp.bfloat16),
+        ],
+        in_specs=[smem] + [hbm] * 5,
+        out_specs=[vmem] * 3,
+        scratch_shapes=[
+            pltpu.VMEM((3, HW, width), jnp.bfloat16),
+            pltpu.VMEM((HW, width), jnp.bfloat16),
+            pltpu.SemaphoreType.DMA((7,)),
+            pltpu.VMEM((clips * slots, width), jnp.bfloat16),
+        ],
+        compiler_params=pltpu.CompilerParams(vmem_limit_bytes=50 * MIB),
+    )(
+        spatial_len,
         latents.reshape(clips * slots, width),
-        w_spatial_qkv,
+        w_spatial_qkv.T,
         w_spatial_out,
-        hbm,
-        55 * MIB,
-        [pltpu.VMEM((clips * slots, width), jnp.bfloat16)],
-    )
-    block = call(
+        w_temporal_qkv.T,
+        w_temporal_out,
+    )
+    block = pl.pallas_call(
         functools.partial(temporal_kernel, clips, slots, groups, frames, each),
-        [frames_len, target],
-        exchange(mid),
-        w_temporal_qkv,
-        w_temporal_out,
-        vmem,
-        51 * MIB,
-        [],
-    )
+        out_shape=pltpu.VMEM(shape, jnp.bfloat16),
+        in_specs=[smem] * 2 + [vmem] * 3,
+        out_specs=vmem,
+        compiler_params=pltpu.CompilerParams(vmem_limit_bytes=40 * MIB),
+    )(frames_len, target, exchange(mid), w_qkv, w_out)
     final = pl.pallas_call(
         functools.partial(crop_kernel, clips),
         out_shape=jax.ShapeDtypeStruct((clips * slots, width), jnp.bfloat16),

time: 104 us -> 103 us (level)
  Pallas kernels: 15.9 us -> 14.8 us
where the time goes in v5:
time: 103 us
  blocking collectives  88.4 us (86%)
  Pallas kernels  14.8 us (14%)
    all_to_all x2, blocking collectives, exchange(): lax.all_to_all(values, ('seq', 'dp'), split_axis=0, concat_axis=0, tiled=...  88.4 us
    pallas_call x1, Pallas kernels, per_device(): pl.pallas_call(functools.partial(spatial_kernel, clips, slots), out_shape...  7.71 us
    pallas_call x1, Pallas kernels, per_device(): pl.pallas_call(functools.partial(temporal_kernel, clips, slots, groups, f...  6.09 us

profile of v5, /device:TPU:1, one launch (start us, length us, event | category | flops | bytes accessed | tf_op | source)
XLA Modules:
  0.0 103.3 jit_solution(178924627794549366)
XLA Ops:
  0.0 7.7 %shard_map.82 = (bf16[256,2,1152]{2,1,0:T(2,128)(2,1)S(1)}, bf16[1728,1152]{1,0:T(8,128)(2,1)S(1)}, bf16[576,1152]{1,0:T(8,128)(2,1)S(1)}) custom-call(s32[224]{0:T(256)} %slen.1, bf16[448,1152]{1,0:T(8,128)(2,1)} %bitcast.8, bf16[1728,1152]{1,0:T(8,128)(2,1)} %bitcast.6, bf16[576,1152]{1,0:T(8,128)(2,1)} %w_out.1, bf16[1728,1152]{1,0:T(8,128)(2,1)} %bitcast.7, ...), custom_call_target="tpu_custom_call" | custom-call | tf_op jit(solution)/shard_map/pallas_call | solution.py:247
  7.7 0.0 copy-start
  7.7 0.0 copy-start.1
  7.7 48.7 %all_to_all.10.x = bf16[256,2,1152]{2,1,0:T(2,128)(2,1)S(1)} all-to-all(bf16[256,2,1152]{2,1,0:T(2,128)(2,1)S(1)} %get-tuple-element.8), channel_id=1, replica_groups=mesh['dp'=32,'seq'=8] {'seq','dp'}, dimensions={0} | all-to-all | bytes 2359296 | tf_op jit(solution)/shard_map/all_to_all | solution.py:238
  56.5 0.0 copy-done
  56.5 0.0 copy-done.1
  56.5 6.1 %shard_map.83 = bf16[256,2,1152]{2,1,0:T(2,128)(2,1)S(1)} custom-call(s32[224]{0:T(256)S(1)} %copy-done, s32[224]{0:T(256)S(1)} %copy-done.1, bf16[256,2,1152]{2,1,0:T(2,128)(2,1)S(1)} %all_to_all.10.x, bf16[1728,1152]{1,0:T(8,128)(2,1)S(1)} %get-tuple-element.9.w_qkv, bf16[576,1152]{1,0:T(8,128)(2,1)S(1)} %get-tuple-element.10.w_out), custom_call_target="tpu_custom_call" | custom-call | tf_op jit(solution)/shard_map/pallas_call | solution.py:271
  62.6 39.6 %all_to_all.11.x = bf16[256,2,1152]{2,1,0:T(2,128)(2,1)S(1)} all-to-all(bf16[256,2,1152]{2,1,0:T(2,128)(2,1)S(1)} %shard_map.83), channel_id=1, replica_groups=mesh['dp'=32,'seq'=8] {'seq','dp'}, dimensions={0} | all-to-all | bytes 2359296 | tf_op jit(solution)/shard_map/all_to_all | solution.py:238
  102.2 1.0 %shard_map.84 = bf16[448,1152]{1,0:T(8,128)(2,1)} custom-call(bf16[256,2,1152]{2,1,0:T(2,128)(2,1)S(1)} %all_to_all.11.x), custom_call_target="tpu_custom_call" | custom-call | tf_op jit(solution)/shard_map/pallas_call | solution.py:278
Async XLA Ops:
  7.7 48.8 %copy-start = (s32[224]{0:T(256)S(1)}, s32[224]{0:T(256)}, u32[]{:S(2)}) copy-start(s32[224]{0:T(256)} %flen.1) | copy-start | bytes 2692
  7.7 48.7 %copy-start.1 = (s32[224]{0:T(256)S(1)}, s32[224]{0:T(256)}, u32[]{:S(2)}) copy-start(s32[224]{0:T(256)} %target.1) | copy-start | bytes 2692

commit v6 on v5

--- a/solution.py
+++ b/solution.py
@@ -60,9 +60,16 @@
             heads.append(jnp.dot(part, weight, preferred_element_type=jnp.float32) * share)
         attn.append(jnp.concatenate(heads, axis=0))
         start = stop
-    attn = jnp.concatenate(attn, axis=1).astype(jnp.bfloat16)
-    block = rows.astype(jnp.float32) + dot(attn, w_out(), COLUMNS_BY_COLUMNS)
-    return block.astype(jnp.bfloat16)
+    back = w_out()
+    block = []
+    start = 0
+    for index in range(0, len(attn), 2):
+        part = jnp.concatenate(attn[index : index + 2], axis=1).astype(jnp.bfloat16)
+        stop = start + part.shape[1]
+        wide = rows[start:stop].astype(jnp.float32) + dot(part, back, COLUMNS_BY_COLUMNS)
+        block.append(wide.astype(jnp.bfloat16))
+        start = stop
+    return jnp.concatenate(block, axis=0)
 
 
 def iotas(size):
@@ -81,8 +88,7 @@
 
     def reader(part):
         def read():
-            for copy in {0: copies[:1], 1: copies[1:]}.get(part, []):
-                copy.wait()
+            copies[part].wait()
             return proj[part] if part < 3 else back[...]
 
         return read
@@ -138,13 +144,13 @@
         pltpu.make_async_copy(next_out, kept_out, sems.at[6]),
     ]
 
-    def keys_weights():
-        held = weights[1]()
+    def values_weights():
+        held = weights[2]()
         for copy in later:
             copy.start()
         return held
 
-    block = attention_part(own[...], weights[0], keys_weights, *weights[2:], biases)
+    block = attention_part(own[...], *weights[:2], values_weights, weights[3], biases)
     out[:filled] = block.reshape(filled, each, width)
     for copy in later:
         copy.wait()
@@ -157,10 +163,11 @@
     slot = jnp.minimum(home * each // slots, clips - 1)
     plane = groups * each
     row, col = iotas(plane)
-    goal = jnp.zeros((plane, plane), jnp.int32)
-    most = jnp.zeros((plane, plane), jnp.int32)
+    owner = lax.broadcasted_iota(jnp.int32, (1, plane), 1) // each
+    goal = jnp.zeros((1, plane), jnp.int32)
+    most = jnp.zeros((1, plane), jnp.int32)
     for group in range(groups):
-        here = col // each == group
+        here = owner == group
         goal = jnp.where(here, target[group * clips + slot] // clips, goal)
         most = jnp.where(here, flen[group * clips + slot], most)
     moved = (goal == row // each) & (row % each == col % each)

time: 103 us -> 103 us (level)
  no operation moved by 1% of the time
where the time goes in v6:
time: 103 us
  blocking collectives  88.4 us (86%)
  Pallas kernels  14.5 us (14%)
    all_to_all x2, blocking collectives, exchange(): lax.all_to_all(values, ('seq', 'dp'), split_axis=0, concat_axis=0, tiled=...  88.4 us
    pallas_call x1, Pallas kernels, per_device(): pl.pallas_call(functools.partial(spatial_kernel, clips, slots), out_shape...  7.53 us
    pallas_call x1, Pallas kernels, per_device(): pl.pallas_call(functools.partial(temporal_kernel, clips, slots, groups, f...  5.94 us

profile of v6, /device:TPU:1, one launch (start us, length us, event | category | flops | bytes accessed | tf_op | source)
XLA Modules:
  0.0 102.9 jit_solution(15822031933735264196)
XLA Ops:
  0.0 7.5 %shard_map.82 = (bf16[256,2,1152]{2,1,0:T(2,128)(2,1)S(1)}, bf16[1728,1152]{1,0:T(8,128)(2,1)S(1)}, bf16[576,1152]{1,0:T(8,128)(2,1)S(1)}) custom-call(s32[224]{0:T(256)} %slen.1, bf16[448,1152]{1,0:T(8,128)(2,1)} %bitcast.8, bf16[1728,1152]{1,0:T(8,128)(2,1)} %bitcast.6, bf16[576,1152]{1,0:T(8,128)(2,1)} %w_out.1, bf16[1728,1152]{1,0:T(8,128)(2,1)} %bitcast.7, ...), custom_call_target="tpu_custom_call" | custom-call | tf_op jit(solution)/shard_map/pallas_call | solution.py:254
  7.5 0.0 copy-start
  7.5 0.0 copy-start.1
  7.6 48.7 %all_to_all.10.x = bf16[256,2,1152]{2,1,0:T(2,128)(2,1)S(1)} all-to-all(bf16[256,2,1152]{2,1,0:T(2,128)(2,1)S(1)} %get-tuple-element.8), channel_id=1, replica_groups=mesh['dp'=32,'seq'=8] {'seq','dp'}, dimensions={0} | all-to-all | bytes 2359296 | tf_op jit(solution)/shard_map/all_to_all | solution.py:245
  56.3 0.0 copy-done
  56.3 0.0 copy-done.1
  56.3 5.9 %shard_map.83 = bf16[256,2,1152]{2,1,0:T(2,128)(2,1)S(1)} custom-call(s32[224]{0:T(256)S(1)} %copy-done, s32[224]{0:T(256)S(1)} %copy-done.1, bf16[256,2,1152]{2,1,0:T(2,128)(2,1)S(1)} %all_to_all.10.x, bf16[1728,1152]{1,0:T(8,128)(2,1)S(1)} %get-tuple-element.9.w_qkv, bf16[576,1152]{1,0:T(8,128)(2,1)S(1)} %get-tuple-element.10.w_out), custom_call_target="tpu_custom_call" | custom-call | tf_op jit(solution)/shard_map/pallas_call | solution.py:278
  62.3 39.6 %all_to_all.11.x = bf16[256,2,1152]{2,1,0:T(2,128)(2,1)S(1)} all-to-all(bf16[256,2,1152]{2,1,0:T(2,128)(2,1)S(1)} %shard_map.83), channel_id=1, replica_groups=mesh['dp'=32,'seq'=8] {'seq','dp'}, dimensions={0} | all-to-all | bytes 2359296 | tf_op jit(solution)/shard_map/all_to_all | solution.py:245
  101.9 1.0 %shard_map.84 = bf16[448,1152]{1,0:T(8,128)(2,1)} custom-call(bf16[256,2,1152]{2,1,0:T(2,128)(2,1)S(1)} %all_to_all.11.x), custom_call_target="tpu_custom_call" | custom-call | tf_op jit(solution)/shard_map/pallas_call | solution.py:285
Async XLA Ops:
  7.5 48.8 %copy-start = (s32[224]{0:T(256)S(1)}, s32[224]{0:T(256)}, u32[]{:S(2)}) copy-start(s32[224]{0:T(256)} %flen.1) | copy-start | bytes 2692
  7.5 48.8 %copy-start.1 = (s32[224]{0:T(256)S(1)}, s32[224]{0:T(256)}, u32[]{:S(2)}) copy-start(s32[224]{0:T(256)} %target.1) | copy-start | bytes 2692

commit v7 on v6

--- a/solution.py
+++ b/solution.py
@@ -96,10 +96,40 @@
     return copies, [reader(part) for part in range(4)]
 
 
+def temporal_plan(clips, slots, groups, frames, each, flen, target, move, mask):
+    home = lax.axis_index("seq") * groups + lax.axis_index("dp")
+    slot = jnp.minimum(home * each // slots, clips - 1)
+    plane = groups * each
+    row, col = iotas(plane)
+    owner = lax.broadcasted_iota(jnp.int32, (1, plane), 1) // each
+    goal = jnp.zeros((1, plane), jnp.int32)
+    most = jnp.zeros((1, plane), jnp.int32)
+    for group in range(groups):
+        here = owner == group
+        goal = jnp.where(here, target[group * clips + slot] // clips, goal)
+        most = jnp.where(here, flen[group * clips + slot], most)
+    moved = (goal == row // each) & (row % each == col % each)
+    most = jnp.sum(jnp.where(moved, most.astype(jnp.float32), 0.0), axis=1, keepdims=True)
+    move[...] = jnp.where(moved, 1.0, 0.0).astype(jnp.bfloat16)
+    part = BLOCK // frames
+    starts = range(0, plane, part)
+    row, col = iotas(BLOCK)
+    same = row % part == col % part
+    frame = (row // part).astype(jnp.float32)
+    for index, start in enumerate(starts):
+        live = jnp.concatenate([most[start : start + part]] * frames, axis=0)
+        mask[index] = jnp.where(same & (frame < live), 0.0, -1e30)
+
+
 def spatial_kernel(
     clips,
     slots,
+    groups,
+    frames,
+    each,
     slen,
+    flen,
+    target,
     x,
     w_qkv,
     w_out,
@@ -108,6 +138,8 @@
     out,
     kept_qkv,
     kept_out,
+    move,
+    mask,
     proj,
     back,
     sems,
@@ -133,9 +165,10 @@
                 & (row < first + slen[group * clips + clip])
             )
         biases.append(jnp.where(live, 0.0, -1e30))
-    each, width = out.shape[1:]
+    width = out.shape[2]
     filled = total // each
     out[filled:] = jnp.zeros((out.shape[0] - filled, each, width), jnp.bfloat16)
+    temporal_plan(clips, slots, groups, frames, each, flen, target, move, mask)
     arrival.wait()
     for copy in copies[1:]:
         copy.start()
@@ -156,23 +189,12 @@
         copy.wait()
 
 
-def temporal_kernel(
-    clips, slots, groups, frames, each, flen, target, x, w_qkv, w_out, out
-):
-    home = lax.axis_index("seq") * groups + lax.axis_index("dp")
-    slot = jnp.minimum(home * each // slots, clips - 1)
+def temporal_kernel(groups, frames, each, x, w_qkv, w_out, move, mask, out):
     plane = groups * each
-    row, col = iotas(plane)
-    owner = lax.broadcasted_iota(jnp.int32, (1, plane), 1) // each
-    goal = jnp.zeros((1, plane), jnp.int32)
-    most = jnp.zeros((1, plane), jnp.int32)
-    for group in range(groups):
-        here = owner == group
-        goal = jnp.where(here, target[group * clips + slot] // clips, goal)
-        most = jnp.where(here, flen[group * clips + slot], most)
-    moved = (goal == row // each) & (row % each == col % each)
-    most = jnp.sum(jnp.where(moved, most.astype(jnp.float32), 0.0), axis=1, keepdims=True)
-    moved = jnp.where(moved, 1.0, 0.0).astype(jnp.bfloat16)
+    part = BLOCK // frames
+    starts = range(0, plane, part)
+    moved = move[...]
+    biases = [mask[index] for index in range(len(starts))]
     planes = [
         jnp.dot(
             moved,
@@ -181,15 +203,6 @@
         ).astype(jnp.bfloat16)
         for frame in range(frames)
     ]
-    part = BLOCK // frames
-    starts = range(0, plane, part)
-    row, col = iotas(BLOCK)
-    same = row % part == col % part
-    frame = (row // part).astype(jnp.float32)
-    biases = []
-    for start in starts:
-        live = jnp.concatenate([most[start : start + part]] * frames, axis=0)
-        biases.append(jnp.where(same & (frame < live), 0.0, -1e30))
     rows = jnp.concatenate([held[start : start + part] for start in starts for held in planes])
     block = attention_part(
         rows,
@@ -251,15 +264,17 @@
         )
 
     shape = (devices, each, width)
-    mid, w_qkv, w_out = pl.pallas_call(
-        functools.partial(spatial_kernel, clips, slots),
+    mid, w_qkv, w_out, move, mask = pl.pallas_call(
+        functools.partial(spatial_kernel, clips, slots, groups, frames, each),
         out_shape=[
             pltpu.VMEM(shape, jnp.bfloat16),
             pltpu.VMEM((3 * HW, width), jnp.bfloat16),
             pltpu.VMEM((HW, width), jnp.bfloat16),
+            pltpu.VMEM((groups * each, groups * each), jnp.bfloat16),
+            pltpu.VMEM((groups * each * frames // BLOCK, BLOCK, BLOCK), jnp.float32),
         ],
-        in_specs=[smem] + [hbm] * 5,
-        out_specs=[vmem] * 3,
+        in_specs=[smem] * 3 + [hbm] * 5,
+        out_specs=[vmem] * 5,
         scratch_shapes=[
             pltpu.VMEM((3, HW, width), jnp.bfloat16),
             pltpu.VMEM((HW, width), jnp.bfloat16),
@@ -269,6 +284,8 @@
         compiler_params=pltpu.CompilerParams(vmem_limit_bytes=50 * MIB),
     )(
         spatial_len,
+        frames_len,
+        target,
         latents.reshape(clips * slots, width),
         w_spatial_qkv.T,
         w_spatial_out,
@@ -276,12 +293,12 @@
         w_temporal_out,
     )
     block = pl.pallas_call(
-        functools.partial(temporal_kernel, clips, slots, groups, frames, each),
+        functools.partial(temporal_kernel, groups, frames, each),
         out_shape=pltpu.VMEM(shape, jnp.bfloat16),
-        in_specs=[smem] * 2 + [vmem] * 3,
+        in_specs=[vmem] * 5,
         out_specs=vmem,
         compiler_params=pltpu.CompilerParams(vmem_limit_bytes=40 * MIB),
-    )(frames_len, target, exchange(mid), w_qkv, w_out)
+    )(exchange(mid), w_qkv, w_out, move, mask)
     final = pl.pallas_call(
         functools.partial(crop_kernel, clips),
         out_shape=jax.ShapeDtypeStruct((clips * slots, width), jnp.bfloat16),

time: 103 us -> 103 us (level)
  no operation moved by 1% of the time
where the time goes in v7:
time: 103 us; the launch traced here: 102 us
  blocking collectives  88.4 us (86%)
  Pallas kernels  13.9 us (13%)
    all_to_all x2, blocking collectives, exchange(): lax.all_to_all(values, ('seq', 'dp'), split_axis=0, concat_axis=0, tiled=...  88.4 us
    pallas_call x1, Pallas kernels, per_device(): pl.pallas_call(functools.partial(spatial_kernel, clips, slots, groups, fr...  7.76 us
    pallas_call x1, Pallas kernels, per_device(): pl.pallas_call(functools.partial(temporal_kernel, groups, frames, each),...  5.14 us

profile of v7, /device:TPU:1, one launch (start us, length us, event | category | flops | bytes accessed | tf_op | source)
XLA Modules:
  0.0 102.3 jit_solution(9178760287623511737)
XLA Ops:
  0.0 7.8 %shard_map.82 = (bf16[256,2,1152]{2,1,0:T(2,128)(2,1)S(1)}, bf16[1728,1152]{1,0:T(8,128)(2,1)S(1)}, bf16[576,1152]{1,0:T(8,128)(2,1)S(1)}, bf16[64,64]{1,0:T(8,128)(2,1)S(1)}, f32[4,128,128]{2,1,0:T(8,128)S(1)}) custom-call(s32[224]{0:T(256)} %slen.1, s32[224]{0:T(256)} %flen.1, s32[224]{0:T(256)} %target.1, bf16[448,1152]{1,0:T(8,128)(2,1)} %bitcast.8, ...), custom_call_target="tpu_custom_call" | custom-call | tf_op jit(solution)/shard_map/pallas_call | solution.py:267
  7.8 48.8 %all_to_all.10.x = bf16[256,2,1152]{2,1,0:T(2,128)(2,1)S(1)} all-to-all(bf16[256,2,1152]{2,1,0:T(2,128)(2,1)S(1)} %get-tuple-element.10), channel_id=1, replica_groups=mesh['dp'=32,'seq'=8] {'seq','dp'}, dimensions={0} | all-to-all | bytes 2359296 | tf_op jit(solution)/shard_map/all_to_all | solution.py:258
  56.5 5.1 %shard_map.83 = bf16[256,2,1152]{2,1,0:T(2,128)(2,1)S(1)} custom-call(bf16[256,2,1152]{2,1,0:T(2,128)(2,1)S(1)} %all_to_all.10.x, bf16[1728,1152]{1,0:T(8,128)(2,1)S(1)} %get-tuple-element.11.w_qkv, bf16[576,1152]{1,0:T(8,128)(2,1)S(1)} %get-tuple-element.12.w_out, bf16[64,64]{1,0:T(8,128)(2,1)S(1)} %get-tuple-element.13.move, ...), custom_call_target="tpu_custom_call" | custom-call | tf_op jit(solution)/shard_map/pallas_call | solution.py:295
  61.7 39.6 %all_to_all.11.x = bf16[256,2,1152]{2,1,0:T(2,128)(2,1)S(1)} all-to-all(bf16[256,2,1152]{2,1,0:T(2,128)(2,1)S(1)} %shard_map.83), channel_id=1, replica_groups=mesh['dp'=32,'seq'=8] {'seq','dp'}, dimensions={0} | all-to-all | bytes 2359296 | tf_op jit(solution)/shard_map/all_to_all | solution.py:258
  101.3 1.0 %shard_map.84 = bf16[448,1152]{1,0:T(8,128)(2,1)} custom-call(bf16[256,2,1152]{2,1,0:T(2,128)(2,1)S(1)} %all_to_all.11.x), custom_call_target="tpu_custom_call" | custom-call | tf_op jit(solution)/shard_map/pallas_call | solution.py:302
